TPU v7x, 32 devices: a whole 2x2x4 slice. The times are simulated.
32 devices in a mesh: dom: 16 (over z, x, core), sub: 2 (over y).
Axes of the slice: x: 2, y: 2, z: 4, core: 2. Of those that a mesh axis runs over, the one named last changes fastest.
Arguments:
- node_features: bfloat16 [65536, 128], P(('dom', 'sub')), may hold values from -6 to 6
- near_fine: int32 [512, 3], P(('dom', 'sub')), may hold values from 0 to 511, as said below
- near_mid: int32 [128, 3], replicated, may hold values from 0 to 127, as said below
- near_top: int32 [32, 3], replicated, may hold values from 0 to 31, as said below
- restrict_mid: int32 [128, 4], replicated, may hold values from 0 to 511, as said below
- restrict_top: int32 [32, 4], replicated, may hold values from 0 to 127, as said below
- node_kernel: bfloat16 [3, 3, 128, 128], replicated, may hold values from -0.5 to 0.5
- channel_kernel: bfloat16 [3, 3, 128, 128], replicated, may hold values from -0.3125 to 0.3125
- restrict_weight: bfloat16 [2, 4, 128, 128], replicated, may hold values from -0.25 to 0.25
- interp_weight: bfloat16 [2, 4, 128, 128], replicated, may hold values from -0.5 to 0.5
- skip_weight: bfloat16 [128, 128], replicated, may hold values from -0.5 to 0.5
Outputs:
- updated: bfloat16 [65536, 128], P(('dom', 'sub'))
Inputs may be any that keep to these rules, and one draw needn't show every extreme that they name: `near_fine`: blocks are numbered region by region along dom+sub, 16 to a device. Row i names in column 0 a block of the same device, in column 1 one of the last 4 blocks of the previous device and in column 2 one of the first 4 blocks of the next device; where that device does not exist, a block of the same device. `near_mid`: A middle-level group is the 16 blocks numbered g * 16 to (g + 1) * 16 - 1 with g = D * 2 + s, D < 16 // 4. Row i of group (D, s) names in column 0 a block of its group, in column 1 one of the last 4 blocks of group (D - 1, s) and in column 2 one of the first 4 blocks of group (D + 1, s); where that group does not exist, a block of its own group. `near_top`: as for near_mid, with groups (D, s), D < 16 // 16, of the coarsest level. `restrict_mid`: row j = (D * 2 + s) * 16 + b lists, in some order, the four blocks ((4 D + r) * 2 + s) * 16 + b for r = 0..3 of the finest level. `restrict_top`: row j = (D * 2 + s) * 16 + b lists, in some order, the four blocks ((4 D + r) * 2 + s) * 16 + b for r = 0..3 of the middle level.
All inputs are finite; a program needn't handle non-finite values.
Results may differ from a plain program's by a relative error of at most 0.0075.
Values may be sent and summed in bfloat16 or wider, within the bound.
A program may use at most 64 MiB of HBM per device.

v0:
```python
import jax
import jax.numpy as jnp
from jax import lax
from jax.sharding import PartitionSpec as P

C = 128
BS = 128
KN = 3
LEVELS = 3
BLK_DEV = 16
HALO_BLK = 4


def padded(x, sides, width):
    for axis, dim in sides:
        count, length = (lax.axis_size(axis), x.shape[dim])
        up = [(i, (i + 1) % count) for i in range(count - 1)]
        down = [(j, i) for i, j in up]
        last = lax.slice_in_dim(x, length - width, length, axis=dim)
        initial = lax.slice_in_dim(x, 0, width, axis=dim)
        before = lax.ppermute(last, axis, up)
        after = lax.ppermute(initial, axis, down)
        x = jnp.concatenate([before, x, after], axis=dim)
    return x


def from_behind(value, axis, steps):
    count = lax.axis_size(axis)
    initial, last = (max(0, -steps), min(count, count - steps))
    return lax.ppermute(value, axis, [(source, source + steps) for source in range(initial, last)])


def partner(x, axis, bit):
    return lax.ppermute(x, axis, [(i, i ^ 1 << bit) for i in range(lax.axis_size(axis))])


def local_slots(near_rows, own_start, pitch_rows):
    lower_start = own_start - pitch_rows
    upper_start = own_start + pitch_rows
    from_lower = near_rows - lower_start - (BLK_DEV - HALO_BLK)
    from_upper = near_rows - upper_start + HALO_BLK + BLK_DEV
    from_own = near_rows - own_start + HALO_BLK
    return jnp.where(
        near_rows < own_start,
        from_lower,
        jnp.where(near_rows >= own_start + BLK_DEV, from_upper, from_own),
    )


def near_term(window, slot_rows, node_mats, chan_mats):
    flat_rows = window.reshape(-1, C)
    summed = jnp.zeros((BLK_DEV, BS, C), jnp.float32)
    for column in range(KN):
        mixed_rows = (
            jnp.dot(flat_rows, chan_mats[column], preferred_element_type=jnp.float32)
            .astype(jnp.bfloat16)
            .reshape(-1, BS, C)
        )
        picked = jnp.take(mixed_rows, slot_rows[:, column], axis=0)
        summed = summed + jnp.einsum(
            "pq,bqc->bpc", node_mats[column], picked, preferred_element_type=jnp.float32
        )
    return summed


def pick_matrices(onehot, matrices):
    return jnp.einsum("bs,spq->bpq", onehot, matrices.astype(jnp.float32)).astype(jnp.bfloat16)


def shards(
    node_features,
    near_fine,
    near_mid,
    near_top,
    restrict_mid,
    restrict_top,
    node_kernel,
    channel_kernel,
    restrict_weight,
    interp_weight,
    skip_weight,
):
    dom_index = lax.axis_index("dom")
    sub_index = lax.axis_index("sub")
    sub_count = lax.axis_size("sub")
    near_lists = (near_fine, near_mid, near_top)
    kid_lists = (restrict_mid, restrict_top)
    current = node_features.reshape(BLK_DEV, BS, C)
    block_range = jnp.arange(BLK_DEV, dtype=jnp.int32)
    half_count = BLK_DEV // 2
    quarter_count = BLK_DEV // 4
    kernels = []
    onehots = []
    for tier_index in range(LEVELS):
        stride = 4**tier_index
        own_start = (dom_index // stride * sub_count + sub_index) * BLK_DEV
        if tier_index == 0:
            window = padded(current, ((("dom", "sub"), 0),), HALO_BLK)
            near_rows = near_fine
            pitch_rows = BLK_DEV
        else:
            lower_rim = from_behind(current[BLK_DEV - HALO_BLK :], "dom", stride)
            upper_rim = from_behind(current[:HALO_BLK], "dom", -stride)
            window = jnp.concatenate([lower_rim, current, upper_rim], axis=0)
            near_rows = lax.dynamic_slice_in_dim(near_lists[tier_index], own_start, BLK_DEV, 0)
            pitch_rows = sub_count * BLK_DEV
        slot_rows = local_slots(near_rows, own_start, pitch_rows)
        kernels.append(
            near_term(window, slot_rows, node_kernel[tier_index], channel_kernel[tier_index])
        )
        if tier_index + 1 < LEVELS:
            parent_start = (dom_index // (4 * stride) * sub_count + sub_index) * BLK_DEV
            parent_rows = lax.dynamic_slice_in_dim(kid_lists[tier_index], parent_start, BLK_DEV, 0)
            own_ids = own_start + block_range
            onehot = (parent_rows == own_ids[:, None]).astype(jnp.float32)
            onehots.append(onehot)
            first_bit = dom_index // stride % 2
            second_bit = dom_index // (2 * stride) % 2
            chosen = pick_matrices(onehot, restrict_weight[tier_index])
            partial_sum = jnp.einsum(
                "bpq,bqc->bpc", chosen, current, preferred_element_type=jnp.float32
            )
            lower_half = partial_sum[:half_count]
            upper_half = partial_sum[half_count:]
            outgoing = jnp.where(first_bit == 0, upper_half, lower_half)
            kept_half = jnp.where(first_bit == 0, lower_half, upper_half) + partner(
                outgoing, "dom", 2 * tier_index
            )
            lower_quarter = kept_half[:quarter_count]
            upper_quarter = kept_half[quarter_count:]
            leaving = jnp.where(second_bit == 0, upper_quarter, lower_quarter)
            kept_quarter = jnp.where(second_bit == 0, lower_quarter, upper_quarter) + partner(
                leaving, "dom", 2 * tier_index + 1
            )
            share = kept_quarter.astype(jnp.bfloat16)
            other_share = partner(share, "dom", 2 * tier_index + 1)
            half_rows = jnp.where(
                second_bit == 0,
                jnp.concatenate([share, other_share]),
                jnp.concatenate([other_share, share]),
            )
            other_half = partner(half_rows, "dom", 2 * tier_index)
            current = jnp.where(
                first_bit == 0,
                jnp.concatenate([half_rows, other_half]),
                jnp.concatenate([other_half, half_rows]),
            )
    upward = kernels[LEVELS - 1]
    for tier_index in range(LEVELS - 2, -1, -1):
        coarse = upward.astype(jnp.bfloat16)
        chosen = pick_matrices(onehots[tier_index], interp_weight[tier_index])
        upward = kernels[tier_index] + jnp.einsum(
            "bpq,bqc->bpc", chosen, coarse, preferred_element_type=jnp.float32
        )
    skip_term = jnp.dot(node_features, skip_weight, preferred_element_type=jnp.float32)
    return jax.nn.gelu(skip_term + upward.reshape(-1, C)).astype(jnp.bfloat16)


def solution(mesh):
    in_specs = (
        P(("dom", "sub"), None),
        P(("dom", "sub"), None),
        P(),
        P(),
        P(),
        P(),
        P(),
        P(),
        P(),
        P(),
        P(),
    )
    out_specs = P(("dom", "sub"), None)
    return jax.shard_map(shards, mesh=mesh, in_specs=in_specs, out_specs=out_specs, check_vma=False)
```

profile of v0, /device:TPU:0, one launch (start us, length us, event | category | flops | bytes accessed | tf_op | source)
XLA Modules:
  0.0 117.2 jit_solution(9470696927608538952)
XLA Ops:
  0.0 1.0 slice_bitcast_fusion
  1.1 0.8 fusion.88
  1.8 0.4 fusion.48
  2.2 0.3 fusion.12
  2.6 0.9 slice_select_fusion.1
  3.5 0.5 collective-permute-start.2
  3.9 4.4 %collective-permute-start = (bf16[4,128,128]{2,1,0:T(8,128)(2,1)S(1)}, bf16[4,128,128]{2,1,0:T(8,128)(2,1)S(1)}, u32[]{:S(2)}, u32[]{:S(2)}) collective-permute-start(bf16[4,128,128]{2,1,0:T(8,128)(2,1)S(1)} %bitcast.171), channel_id=1, source_target_pairs={{0,1},{1,2},{2,3},{3,4},{4,5},{5,6},{6,7},{7,8},{8,9},{9,10},{10,1... | collective-permute-start | bytes 393224 | tf_op jit(solution)/shard_map/ppermute | solution.py:21
  8.4 1.3 %collective-permute-start.1 = (bf16[4,128,128]{2,1,0:T(8,128)(2,1)S(1)}, bf16[4,128,128]{2,1,0:T(8,128)(2,1)S(1)}, u32[]{:S(2)}, u32[]{:S(2)}) collective-permute-start(bf16[4,128,128]{2,1,0:T(8,128)(2,1)S(1)} %bitcast.170), channel_id=1, source_target_pairs={{1,0},{2,1},{3,2},{4,3},{5,4},{6,5},{7,6},{8,7},{9,8},{10,9},{11,1... | collective-permute-start | bytes 393224 | tf_op jit(solution)/shard_map/ppermute | solution.py:22
  10.2 1.2 %fusion.44 = bf16[16,128,128]{2,0,1:T(8,128)(2,1)} fusion(pred[16,4,1]{0,1,2:T(4,128)(4,1)S(1)} %fusion.89, bf16[4,128,128]{2,1,0:T(8,128)(2,1)S(1)} %get-tuple-element.32), kind=kOutput, calls=%fused_computation.91 | convolution fusion | flops 2097152 | bytes 655424 | tf_op jit(solution)/shard_map/bs,spq->bpq/dot_general | solution.py:67
  11.3 1.2 %fusion.46 = bf16[16,128,128]{2,0,1:T(8,128)(2,1)} fusion(pred[16,4,1]{0,1,2:T(4,128)(4,1)S(1)} %fusion.89, bf16[4,128,128]{2,1,0:T(8,128)(2,1)S(1)} %get-tuple-element.30), kind=kOutput, calls=%fused_computation.93 | convolution fusion | flops 2097152 | bytes 655424 | tf_op jit(solution)/shard_map/bs,spq->bpq/dot_general | solution.py:67
  12.5 1.2 %fusion.50 = bf16[16,128,128]{2,0,1:T(8,128)(2,1)} fusion(pred[16,4,1]{0,1,2:T(4,128)(4,1)S(1)} %fusion.88, bf16[4,128,128]{2,1,0:T(8,128)(2,1)S(1)} %get-tuple-element.31), kind=kOutput, calls=%fused_computation.97 | convolution fusion | flops 2097152 | bytes 655424 | tf_op jit(solution)/shard_map/bs,spq->bpq/dot_general | solution.py:67
  13.8 2.1 %collective-permute-done.1 = bf16[4,128,128]{2,1,0:T(8,128)(2,1)S(1)} collective-permute-done((bf16[4,128,128]{2,1,0:T(8,128)(2,1)S(1)}, bf16[4,128,128]{2,1,0:T(8,128)(2,1)S(1)}, u32[]{:S(2)}, u32[]{:S(2)}) %collective-permute-start.1) | collective-permute-done | bytes 131104 | tf_op jit(solution)/shard_map/ppermute | solution.py:22
  16.0 1.1 convolution_convert_fusion.7
  17.1 1.4 %gather_fusion.1 = bf16[16,128,128]{2,1,0:T(8,128)(2,1)} fusion(bf16[24,128,128]{2,1,0:T(8,128)(2,1)S(1)} %bitcast.166, s32[1024]{0:T(1024)S(1)} %get-tuple-element.53), kind=kCustom, calls=%fused_computation.1.clone | custom fusion | bytes 1048640 | tf_op jit(solution)/shard_map/jit(_take)/gather | solution.py:59
  18.5 1.1 convolution_convert_fusion.8
  19.6 1.4 %gather_fusion = bf16[16,128,128]{2,1,0:T(8,128)(2,1)} fusion(bf16[24,128,128]{2,1,0:T(8,128)(2,1)S(1)} %bitcast.167, s32[1024]{0:T(1024)S(1)} %pad_clamp_fusion.8), kind=kCustom, calls=%fused_computation.clone | custom fusion | bytes 1048640 | tf_op jit(solution)/shard_map/jit(_take)/gather | solution.py:59
  21.0 1.4 %fusion.24 = f32[16,128,128]{1,2,0:T(8,128)S(1)} fusion(bf16[16,128,128]{2,1,0:T(8,128)(2,1)} %gather_fusion, pred[16]{0:T(512)(128)(4,1)S(1)} %get-tuple-element.44, bf16[3,3,128,128]{3,2,1,0:T(8,128)(2,1)} %param.19), kind=kOutput, calls=%fused_computation.61 | convolution fusion | flops 67371008 | bytes 1605648 | tf_op jit(solution)/shard_map/pq,bqc->bpc/dot_general | solution.py:60
  22.5 1.2 %select_add_fusion.1 = f32[8,128,128]{2,1,0:T(8,128)S(1)} fusion(f32[8,128,128]{2,1,0:T(8,128)} %collective-permute-done.2, f32[16,128,128]{2,1,0:T(8,128)S(1)} %fusion.12, pred[]{:T(512)S(6)} %eq.43), kind=kLoop, calls=%fused_computation.64 | loop fusion | flops 262144 | bytes 2097153 | tf_op jit(solution)/shard_map/add | solution.py:126
  23.7 1.8 %collective-permute-start.3 = (f32[4,128,128]{2,1,0:T(8,128)S(1)}, f32[4,128,128]{2,1,0:T(8,128)S(1)}, u32[]{:S(2)}, u32[]{:S(2)}) collective-permute-start(f32[4,128,128]{2,1,0:T(8,128)S(1)} %slice_select_fusion.3), channel_id=1, source_target_pairs={{0,4},{2,6},{4,0},{6,2},{8,12},{10,14},{12,8},{14,10},{16,20},{18,... | collective-permute-start | bytes 786440 | tf_op jit(solution)/shard_map/ppermute | solution.py:34
  25.5 1.1 convolution_add_fusion.6
  26.6 5.0 %collective-permute-done.3 = f32[4,128,128]{2,1,0:T(8,128)S(1)} collective-permute-done((f32[4,128,128]{2,1,0:T(8,128)S(1)}, f32[4,128,128]{2,1,0:T(8,128)S(1)}, u32[]{:S(2)}, u32[]{:S(2)}) %collective-permute-start.3) | collective-permute-done | bytes 262176 | tf_op jit(solution)/shard_map/ppermute | solution.py:34
  31.6 1.8 %collective-permute-start.4 = (bf16[4,128,128]{2,1,0:T(8,128)(2,1)S(1)}, bf16[4,128,128]{2,1,0:T(8,128)(2,1)S(1)}, u32[]{:S(2)}, u32[]{:S(2)}) collective-permute-start(bf16[4,128,128]{2,1,0:T(8,128)(2,1)S(1)} %add_convert_fusion.1), channel_id=1, source_target_pairs={{0,4},{2,6},{4,0},{6,2},{8,12},{10,14},{12,8},{14,10},{16,20},{18,... | collective-permute-start | bytes 393224 | tf_op jit(solution)/shard_map/ppermute | solution.py:34
  33.4 1.1 convolution_convert_fusion.6
  34.6 0.6 gather_fusion.2
  35.2 1.5 %collective-permute-done.4 = bf16[4,128,128]{2,1,0:T(8,128)(2,1)S(1)} collective-permute-done((bf16[4,128,128]{2,1,0:T(8,128)(2,1)S(1)}, bf16[4,128,128]{2,1,0:T(8,128)(2,1)S(1)}, u32[]{:S(2)}, u32[]{:S(2)}) %collective-permute-start.4) | collective-permute-done | bytes 131104 | tf_op jit(solution)/shard_map/ppermute | solution.py:34
  36.8 2.1 %fusion.1 = f32[16,128,128]{2,1,0:T(8,128)} fusion(f32[16,128,128]{1,2,0:T(8,128)S(1)} %convolution_add_fusion.6, bf16[16,128,128]{2,1,0:T(8,128)(2,1)S(1)} %gather_fusion.2, pred[16]{0:T(512)(128)(4,1)S(1)} %get-tuple-element.18, bf16[3,3,128,128]{3,2,1,0:T(8,128)(2,1)} %param.19), kind=kOutput, calls=%fused_computation.26 | convolution fusion | flops 67633152 | bytes 2654224 | tf_op jit(solution)/shard_map/pq,bqc->bpc/dot_general | solution.py:60
  39.0 0.9 copy-done.5
  39.9 0.3 fusion.13
  40.2 3.7 %collective-permute-start.6 = (bf16[4,128,128]{2,1,0:T(8,128)(2,1)S(1)}, bf16[4,128,128]{2,1,0:T(8,128)(2,1)S(1)}, u32[]{:S(2)}, u32[]{:S(2)}) collective-permute-start(bf16[4,128,128]{2,1,0:T(8,128)(2,1)S(1)} %get-tuple-element.26), channel_id=1, source_target_pairs={{0,8},{2,10},{4,12},{6,14},{8,16},{10,18},{12,20},{14,22},{16,24},... | collective-permute-start | bytes 393224 | tf_op jit(solution)/shard_map/ppermute | solution.py:30
  44.0 1.3 %collective-permute-start.7 = (bf16[4,128,128]{2,1,0:T(8,128)(2,1)S(1)}, bf16[4,128,128]{2,1,0:T(8,128)(2,1)S(1)}, u32[]{:S(2)}, u32[]{:S(2)}) collective-permute-start(bf16[4,128,128]{2,1,0:T(8,128)(2,1)S(1)} %get-tuple-element.27), channel_id=1, source_target_pairs={{8,0},{10,2},{12,4},{14,6},{16,8},{18,10},{20,12},{22,14},{24,16},... | collective-permute-start | bytes 393224 | tf_op jit(solution)/shard_map/ppermute | solution.py:30
  45.3 0.9 slice_select_fusion
  46.1 2.6 %collective-permute-start.8 = (f32[8,128,128]{2,1,0:T(8,128)}, f32[8,128,128]{2,1,0:T(8,128)}, u32[]{:S(2)}, u32[]{:S(2)}) collective-permute-start(f32[8,128,128]{2,1,0:T(8,128)} %slice_select_fusion), channel_id=1, source_target_pairs={{0,8},{2,10},{4,12},{6,14},{8,0},{10,2},{12,4},{14,6},{16,24},{18,... | collective-permute-start | bytes 1572872 | tf_op jit(solution)/shard_map/ppermute | solution.py:34
  48.8 3.4 %collective-permute-done.7 = bf16[4,128,128]{2,1,0:T(8,128)(2,1)S(1)} collective-permute-done((bf16[4,128,128]{2,1,0:T(8,128)(2,1)S(1)}, bf16[4,128,128]{2,1,0:T(8,128)(2,1)S(1)}, u32[]{:S(2)}, u32[]{:S(2)}) %collective-permute-start.7) | collective-permute-done | bytes 131104 | tf_op jit(solution)/shard_map/ppermute | solution.py:30
  52.3 1.1 convolution_convert_fusion.5
  53.4 1.4 %gather_fusion.3 = bf16[16,128,128]{2,1,0:T(8,128)(2,1)} fusion(bf16[24,128,128]{2,1,0:T(8,128)(2,1)S(1)} %bitcast.168, s32[1024]{0:T(1024)S(1)} %pad_clamp_fusion.5), kind=kCustom, calls=%fused_computation.3.clone | custom fusion | bytes 1048640 | tf_op jit(solution)/shard_map/jit(_take)/gather | solution.py:59
  54.8 1.4 %fusion.20 = f32[16,128,128]{1,2,0:T(8,128)S(1)} fusion(bf16[16,128,128]{2,1,0:T(8,128)(2,1)} %gather_fusion.3, pred[16]{0:T(512)(128)(4,1)S(1)} %get-tuple-element.46, bf16[3,3,128,128]{3,2,1,0:T(8,128)(2,1)} %param.19), kind=kOutput, calls=%fused_computation.57 | convolution fusion | flops 67371008 | bytes 1605648 | tf_op jit(solution)/shard_map/pq,bqc->bpc/dot_general | solution.py:60
  56.2 6.6 %collective-permute-done.8 = f32[8,128,128]{2,1,0:T(8,128)} collective-permute-done((f32[8,128,128]{2,1,0:T(8,128)}, f32[8,128,128]{2,1,0:T(8,128)}, u32[]{:S(2)}, u32[]{:S(2)}) %collective-permute-start.8) | collective-permute-done | bytes 524320 | tf_op jit(solution)/shard_map/ppermute | solution.py:34
  62.8 1.1 select_add_fusion
  64.0 2.7 %collective-permute-start.9 = (f32[4,128,128]{2,1,0:T(8,128)S(1)}, f32[4,128,128]{2,1,0:T(8,128)S(1)}, u32[]{:S(2)}, u32[]{:S(2)}) collective-permute-start(f32[4,128,128]{2,1,0:T(8,128)S(1)} %slice_select_fusion.2), channel_id=1, source_target_pairs={{0,16},{2,18},{4,20},{6,22},{8,24},{10,26},{12,28},{14,30},{16,0},... | collective-permute-start | bytes 786440 | tf_op jit(solution)/shard_map/ppermute | solution.py:34
  66.6 1.1 convolution_convert_fusion.4
  67.7 9.6 %collective-permute-done.9 = f32[4,128,128]{2,1,0:T(8,128)S(1)} collective-permute-done((f32[4,128,128]{2,1,0:T(8,128)S(1)}, f32[4,128,128]{2,1,0:T(8,128)S(1)}, u32[]{:S(2)}, u32[]{:S(2)}) %collective-permute-start.9) | collective-permute-done | bytes 262176 | tf_op jit(solution)/shard_map/ppermute | solution.py:34
  77.3 0.7 add_convert_fusion
  78.0 2.0 %convolution_convert_fusion.3 = bf16[3072,128]{1,0:T(8,128)(2,1)} fusion(bf16[3072,128]{1,0:T(8,128)(2,1)S(1)} %bitcast.154, bf16[3,3,128,128]{3,2,1,0:T(8,128)(2,1)} %param.20), kind=kOutput, calls=%fused_computation.12 | convolution fusion | flops 101056512 | bytes 1605632 | tf_op jit(solution)/shard_map/dot_general | solution.py:55
  80.0 1.4 %gather_fusion.4 = bf16[16,128,128]{2,1,0:T(8,128)(2,1)} fusion(bf16[24,128,128]{2,1,0:T(8,128)(2,1)S(1)} %bitcast.160, s32[1024]{0:T(1024)S(1)} %pad_clamp_fusion.4), kind=kCustom, calls=%fused_computation.4.clone | custom fusion | bytes 1048640 | tf_op jit(solution)/shard_map/jit(_take)/gather | solution.py:59
  81.4 0.6 gather_fusion.5
  82.0 4.0 %collective-permute-done.10 = bf16[4,128,128]{2,1,0:T(8,128)(2,1)} collective-permute-done((bf16[4,128,128]{2,1,0:T(8,128)(2,1)}, bf16[4,128,128]{2,1,0:T(8,128)(2,1)}, u32[]{:S(2)}, u32[]{:S(2)}) %collective-permute-start.10) | collective-permute-done | bytes 131104 | tf_op jit(solution)/shard_map/ppermute | solution.py:34
  86.0 1.1 maximum_select_fusion.3
  87.3 1.4 %convolution_add_fusion.4 = f32[16,128,128]{1,2,0:T(8,128)S(1)} fusion(f32[16,128,128]{1,2,0:T(8,128)S(1)} %fusion.20, bf16[16,128,128]{2,1,0:T(8,128)(2,1)} %gather_fusion.4, pred[16]{0:T(512)(128)(4,1)S(1)} %get-tuple-element.48, bf16[3,3,128,128]{3,2,1,0:T(8,128)(2,1)} %param.19), kind=kOutput, calls=%fused_computation.24 | convolution fusion | flops 67633152 | bytes 2654224 | tf_op jit(solution)/shard_map/pq,bqc->bpc/dot_general | solution.py:60
  88.7 6.2 %collective-permute-done.11 = bf16[8,128,128]{2,1,0:T(8,128)(2,1)S(1)} collective-permute-done((bf16[8,128,128]{2,1,0:T(8,128)(2,1)S(1)}, bf16[8,128,128]{2,1,0:T(8,128)(2,1)S(1)}, u32[]{:S(2)}, u32[]{:S(2)}) %collective-permute-start.11) | collective-permute-done | bytes 262176 | tf_op jit(solution)/shard_map/ppermute | solution.py:34
  95.0 0.7 collective-permute-start.12
  95.6 0.7 collective-permute-start.13
  96.3 1.1 fusion
  97.5 0.1 pad_maximum_fusion.2
  97.6 1.1 convolution_convert_fusion.2
  98.7 2.0 %convolution_convert_fusion.1 = bf16[3072,128]{1,0:T(8,128)(2,1)} fusion(bf16[3072,128]{1,0:T(8,128)(2,1)S(1)} %bitcast.156, bf16[3,3,128,128]{3,2,1,0:T(8,128)(2,1)} %param.20), kind=kOutput, calls=%fused_computation.10 | convolution fusion | flops 101056512 | bytes 1605632 | tf_op jit(solution)/shard_map/dot_general | solution.py:55
  100.7 1.1 convolution_convert_fusion
  101.8 1.4 %gather_fusion.6 = bf16[16,128,128]{2,1,0:T(8,128)(2,1)} fusion(bf16[24,128,128]{2,1,0:T(8,128)(2,1)S(1)} %bitcast.164, s32[1024]{0:T(1024)S(1)} %pad_clamp_fusion.2), kind=kCustom, calls=%fused_computation.6.clone | custom fusion | bytes 1048640 | tf_op jit(solution)/shard_map/jit(_take)/gather | solution.py:59
  103.2 1.6 %fusion.16 = f32[16,128,128]{2,1,0:T(8,128)S(1)} fusion(bf16[16,128,128]{2,1,0:T(8,128)(2,1)} %gather_fusion.6, pred[16]{0:T(512)(128)(4,1)S(1)} %get-tuple-element.36, bf16[3,3,128,128]{3,2,1,0:T(8,128)(2,1)} %param.19), kind=kOutput, calls=%fused_computation.53 | convolution fusion | flops 67371008 | bytes 1605648 | tf_op jit(solution)/shard_map/pq,bqc->bpc/dot_general | solution.py:60
  104.8 2.5 %gather_fusion.7 = bf16[16,128,128]{2,1,0:T(8,128)(2,1)} fusion(bf16[24,128,128]{2,1,0:T(8,128)(2,1)} %bitcast.162, s32[1024]{0:T(1024)S(1)} %pad_clamp_fusion.1), kind=kCustom, calls=%fused_computation.7.clone | custom fusion | bytes 1048640 | tf_op jit(solution)/shard_map/jit(_take)/gather | solution.py:59
  107.3 1.4 %gather_fusion.8 = bf16[16,128,128]{2,1,0:T(8,128)(2,1)} fusion(bf16[24,128,128]{2,1,0:T(8,128)(2,1)S(1)} %bitcast.161, s32[1024]{0:T(1024)S(1)} %pad_clamp_fusion), kind=kCustom, calls=%fused_computation.8.clone | custom fusion | bytes 1048640 | tf_op jit(solution)/shard_map/jit(_take)/gather | solution.py:59
  108.7 1.6 %convolution_add_fusion.8 = f32[16,128,128]{2,1,0:T(8,128)S(1)} fusion(f32[16,128,128]{2,1,0:T(8,128)S(1)} %fusion.16, bf16[16,128,128]{2,1,0:T(8,128)(2,1)} %gather_fusion.7, pred[16]{0:T(512)(128)(4,1)S(1)} %get-tuple-element.34, bf16[3,3,128,128]{3,2,1,0:T(8,128)(2,1)} %param.19), kind=kOutput, calls=%fused_computation.29 | convolution fusion | flops 67633152 | bytes 2654224 | tf_op jit(solution)/shard_map/pq,bqc->bpc/dot_general | solution.py:60
  110.4 1.4 %fusion.2 = bf16[16,128,128]{2,1,0:T(8,128)(2,1)S(1)} fusion(f32[16,128,128]{2,1,0:T(8,128)S(1)} %convolution_add_fusion.8, bf16[16,128,128]{2,1,0:T(8,128)(2,1)S(1)} %copy-done.4, pred[16]{0:T(512)(128)(4,1)S(1)} %get-tuple-element.6, bf16[3,3,128,128]{3,2,1,0:T(8,128)(2,1)} %param.19), kind=kOutput, calls=%fused_computation.30 | convolution fusion | flops 67895296 | bytes 2129936 | tf_op jit(solution)/shard_map/pq,bqc->bpc/dot_general | solution.py:60
  111.8 2.8 %convolution_add_fusion.1 = f32[16,128,128]{2,1,0:T(8,128)} fusion(f32[16,128,128]{2,1,0:T(8,128)S(1)} %copy-done.1, f32[16,128,128]{2,1,0:T(8,128)S(1)} %fusion, bf16[16,128,128]{2,1,0:T(8,128)(2,1)S(1)} %fusion.2, bf16[16,128,128]{2,0,1:T(8,128)(2,1)} %fusion.50, bf16[16,128,128]{2,0,1:T(8,128)(2,1)} %fusion.46), kind=kOutput, calls=%fused_computation.20 | convolution fusion | flops 135004160 | bytes 4718592 | tf_op jit(solution)/shard_map/bpq,bqc->bpc/dot_general | solution.py:152
  114.6 2.5 %fusion.11 = bf16[2048,128]{1,0:T(8,128)(2,1)} fusion(f32[2048,128]{1,0:T(8,128)} %bitcast.169, bf16[2048,128]{1,0:T(8,128)(2,1)S(1)} %copy-done.2, bf16[128,128]{1,0:T(8,128)(2,1)S(1)} %copy-done), kind=kOutput, calls=%fused_computation.39 | convolution fusion | flops 69730304 | bytes 2129920 | tf_op jit(solution)/shard_map/dot_general | solution.py:155
  (60 shorter events, 1.1 us)
Async XLA Ops:
  0.0 114.6 %copy-start = (bf16[128,128]{1,0:T(8,128)(2,1)S(1)}, bf16[128,128]{1,0:T(8,128)(2,1)}, u32[]{:S(2)}) copy-start(bf16[128,128]{1,0:T(8,128)(2,1)} %param.23) | copy-start | bytes 98308
  0.0 2.2 %copy-start.2 = (bf16[2048,128]{1,0:T(8,128)(2,1)S(1)}, bf16[2048,128]{1,0:T(8,128)(2,1)}, u32[]{:S(2)}) copy-start(bf16[2048,128]{1,0:T(8,128)(2,1)} %param.13) | copy-start | bytes 1572868
  2.5 7.2 %copy-start.9 = (s32[32,3]{0,1:T(4,128)S(1)}, s32[32,3]{0,1:T(4,128)}, u32[]{:S(2)}) copy-start(s32[32,3]{0,1:T(4,128)} %param.16) | copy-start | bytes 1156
  2.5 7.2 %copy-start.10 = (s32[128,3]{0,1:T(4,128)S(1)}, s32[128,3]{0,1:T(4,128)}, u32[]{:S(2)}) copy-start(s32[128,3]{0,1:T(4,128)} %param.15) | copy-start | bytes 4612
  2.6 7.4 %copy-start.11 = (s32[16,3]{0,1:T(4,128)S(1)}, s32[16,3]{0,1:T(4,128)}, u32[]{:S(2)}) copy-start(s32[16,3]{0,1:T(4,128)} %param.14) | copy-start | bytes 580
  2.6 7.5 %copy-start.7 = (bf16[2,4,128,128]{3,2,1,0:T(8,128)(2,1)S(1)}, bf16[2,4,128,128]{3,2,1,0:T(8,128)(2,1)}, u32[]{:S(2)}) copy-start(bf16[2,4,128,128]{3,2,1,0:T(8,128)(2,1)} %param.22) | copy-start | bytes 786436
  2.6 7.5 %copy-start.8 = (s32[32,4]{0,1:T(4,128)S(1)}, s32[32,4]{0,1:T(4,128)}, u32[]{:S(2)}) copy-start(s32[32,4]{0,1:T(4,128)} %param.18) | copy-start | bytes 1540
  3.5 19.0 %collective-permute-start.2 = (f32[8,128,128]{2,1,0:T(8,128)}, f32[8,128,128]{2,1,0:T(8,128)}, u32[]{:S(2)}, u32[]{:S(2)}) collective-permute-start(f32[8,128,128]{2,1,0:T(8,128)} %slice_select_fusion.1), channel_id=1, source_target_pairs={{0,2},{2,0},{4,6},{6,4},{8,10},{10,8},{12,14},{14,12},{16,18},{18,... | collective-permute-start | bytes 1572872 | tf_op jit(solution)/shard_map/ppermute | solution.py:34
  3.9 9.8 %collective-permute-start = (bf16[4,128,128]{2,1,0:T(8,128)(2,1)S(1)}, bf16[4,128,128]{2,1,0:T(8,128)(2,1)S(1)}, u32[]{:S(2)}, u32[]{:S(2)}) collective-permute-start(bf16[4,128,128]{2,1,0:T(8,128)(2,1)S(1)} %bitcast.171), channel_id=1, source_target_pairs={{0,1},{1,2},{2,3},{3,4},{4,5},{5,6},{6,7},{7,8},{8,9},{9,10},{10,1... | collective-permute-start | bytes 393224 | tf_op jit(solution)/shard_map/ppermute | solution.py:21
  8.4 7.5 %collective-permute-start.1 = (bf16[4,128,128]{2,1,0:T(8,128)(2,1)S(1)}, bf16[4,128,128]{2,1,0:T(8,128)(2,1)S(1)}, u32[]{:S(2)}, u32[]{:S(2)}) collective-permute-start(bf16[4,128,128]{2,1,0:T(8,128)(2,1)S(1)} %bitcast.170), channel_id=1, source_target_pairs={{1,0},{2,1},{3,2},{4,3},{5,4},{6,5},{7,6},{8,7},{9,8},{10,9},{11,1... | collective-permute-start | bytes 393224 | tf_op jit(solution)/shard_map/ppermute | solution.py:22
  22.5 3.0 %copy-start.6 = (bf16[16,128,128]{2,1,0:T(8,128)(2,1)S(1)}, bf16[16,128,128]{2,1,0:T(8,128)(2,1)}, u32[]{:S(2)}) copy-start(bf16[16,128,128]{2,1,0:T(8,128)(2,1)} %gather_fusion.1) | copy-start | bytes 1572868
  23.7 7.9 %collective-permute-start.3 = (f32[4,128,128]{2,1,0:T(8,128)S(1)}, f32[4,128,128]{2,1,0:T(8,128)S(1)}, u32[]{:S(2)}, u32[]{:S(2)}) collective-permute-start(f32[4,128,128]{2,1,0:T(8,128)S(1)} %slice_select_fusion.3), channel_id=1, source_target_pairs={{0,4},{2,6},{4,0},{6,2},{8,12},{10,14},{12,8},{14,10},{16,20},{18,... | collective-permute-start | bytes 786440 | tf_op jit(solution)/shard_map/ppermute | solution.py:34
  31.6 5.0 %collective-permute-start.4 = (bf16[4,128,128]{2,1,0:T(8,128)(2,1)S(1)}, bf16[4,128,128]{2,1,0:T(8,128)(2,1)S(1)}, u32[]{:S(2)}, u32[]{:S(2)}) collective-permute-start(bf16[4,128,128]{2,1,0:T(8,128)(2,1)S(1)} %add_convert_fusion.1), channel_id=1, source_target_pairs={{0,4},{2,6},{4,0},{6,2},{8,12},{10,14},{12,8},{14,10},{16,20},{18,... | collective-permute-start | bytes 393224 | tf_op jit(solution)/shard_map/ppermute | solution.py:34
  36.7 2.2 %collective-permute-start.5 = (bf16[8,128,128]{2,1,0:T(8,128)(2,1)S(1)}, bf16[8,128,128]{2,1,0:T(8,128)(2,1)S(1)}, u32[]{:S(2)}, u32[]{:S(2)}) collective-permute-start(bf16[8,128,128]{2,1,0:T(8,128)(2,1)S(1)} %maximum_select_fusion.2), channel_id=1, source_target_pairs={{0,2},{2,0},{4,6},{6,4},{8,10},{10,8},{12,14},{14,12},{16,18},{18,... | collective-permute-start | bytes 786440 | tf_op jit(solution)/shard_map/ppermute | solution.py:34
  38.9 1.0 copy-start.5
  40.2 8.5 %collective-permute-start.6 = (bf16[4,128,128]{2,1,0:T(8,128)(2,1)S(1)}, bf16[4,128,128]{2,1,0:T(8,128)(2,1)S(1)}, u32[]{:S(2)}, u32[]{:S(2)}) collective-permute-start(bf16[4,128,128]{2,1,0:T(8,128)(2,1)S(1)} %get-tuple-element.26), channel_id=1, source_target_pairs={{0,8},{2,10},{4,12},{6,14},{8,16},{10,18},{12,20},{14,22},{16,24},... | collective-permute-start | bytes 393224 | tf_op jit(solution)/shard_map/ppermute | solution.py:30
  44.0 8.2 %collective-permute-start.7 = (bf16[4,128,128]{2,1,0:T(8,128)(2,1)S(1)}, bf16[4,128,128]{2,1,0:T(8,128)(2,1)S(1)}, u32[]{:S(2)}, u32[]{:S(2)}) collective-permute-start(bf16[4,128,128]{2,1,0:T(8,128)(2,1)S(1)} %get-tuple-element.27), channel_id=1, source_target_pairs={{8,0},{10,2},{12,4},{14,6},{16,8},{18,10},{20,12},{22,14},{24,16},... | collective-permute-start | bytes 393224 | tf_op jit(solution)/shard_map/ppermute | solution.py:30
  46.1 16.7 %collective-permute-start.8 = (f32[8,128,128]{2,1,0:T(8,128)}, f32[8,128,128]{2,1,0:T(8,128)}, u32[]{:S(2)}, u32[]{:S(2)}) collective-permute-start(f32[8,128,128]{2,1,0:T(8,128)} %slice_select_fusion), channel_id=1, source_target_pairs={{0,8},{2,10},{4,12},{6,14},{8,0},{10,2},{12,4},{14,6},{16,24},{18,... | collective-permute-start | bytes 1572872 | tf_op jit(solution)/shard_map/ppermute | solution.py:34
  64.0 13.3 %collective-permute-start.9 = (f32[4,128,128]{2,1,0:T(8,128)S(1)}, f32[4,128,128]{2,1,0:T(8,128)S(1)}, u32[]{:S(2)}, u32[]{:S(2)}) collective-permute-start(f32[4,128,128]{2,1,0:T(8,128)S(1)} %slice_select_fusion.2), channel_id=1, source_target_pairs={{0,16},{2,18},{4,20},{6,22},{8,24},{10,26},{12,28},{14,30},{16,0},... | collective-permute-start | bytes 786440 | tf_op jit(solution)/shard_map/ppermute | solution.py:34
  78.0 8.0 %collective-permute-start.10 = (bf16[4,128,128]{2,1,0:T(8,128)(2,1)}, bf16[4,128,128]{2,1,0:T(8,128)(2,1)}, u32[]{:S(2)}, u32[]{:S(2)}) collective-permute-start(bf16[4,128,128]{2,1,0:T(8,128)(2,1)} %add_convert_fusion), channel_id=1, source_target_pairs={{0,16},{2,18},{4,20},{6,22},{8,24},{10,26},{12,28},{14,30},{16,0},... | collective-permute-start | bytes 393224 | tf_op jit(solution)/shard_map/ppermute | solution.py:34
  80.0 1.4 %copy-start.3 = (bf16[3072,128]{1,0:T(8,128)(2,1)S(1)}, bf16[3072,128]{1,0:T(8,128)(2,1)}, u32[]{:S(2)}) copy-start(bf16[3072,128]{1,0:T(8,128)(2,1)} %convolution_convert_fusion.3) | copy-start | bytes 2359300
  87.2 7.7 %collective-permute-start.11 = (bf16[8,128,128]{2,1,0:T(8,128)(2,1)S(1)}, bf16[8,128,128]{2,1,0:T(8,128)(2,1)S(1)}, u32[]{:S(2)}, u32[]{:S(2)}) collective-permute-start(bf16[8,128,128]{2,1,0:T(8,128)(2,1)S(1)} %maximum_select_fusion.3), channel_id=1, source_target_pairs={{0,8},{2,10},{4,12},{6,14},{8,0},{10,2},{12,4},{14,6},{16,24},{18,... | collective-permute-start | bytes 786440 | tf_op jit(solution)/shard_map/ppermute | solution.py:34
  95.0 2.5 %collective-permute-start.12 = (bf16[4,128,128]{2,1,0:T(8,128)(2,1)S(1)}, bf16[4,128,128]{2,1,0:T(8,128)(2,1)S(1)}, u32[]{:S(2)}, u32[]{:S(2)}) collective-permute-start(bf16[4,128,128]{2,1,0:T(8,128)(2,1)S(1)} %get-tuple-element.24), channel_id=1, source_target_pairs={} | collective-permute-start | bytes 393224 | tf_op jit(solution)/shard_map/ppermute | solution.py:30
  95.6 1.8 %collective-permute-start.13 = (bf16[4,128,128]{2,1,0:T(8,128)(2,1)S(1)}, bf16[4,128,128]{2,1,0:T(8,128)(2,1)S(1)}, u32[]{:S(2)}, u32[]{:S(2)}) collective-permute-start(bf16[4,128,128]{2,1,0:T(8,128)(2,1)S(1)} %get-tuple-element.25), channel_id=1, source_target_pairs={} | collective-permute-start | bytes 393224 | tf_op jit(solution)/shard_map/ppermute | solution.py:30
  108.7 1.6 %copy-start.4 = (bf16[16,128,128]{2,1,0:T(8,128)(2,1)S(1)}, bf16[16,128,128]{2,1,0:T(8,128)(2,1)}, u32[]{:S(2)}) copy-start(bf16[16,128,128]{2,1,0:T(8,128)(2,1)} %gather_fusion.8) | copy-start | bytes 1572868
  110.4 1.4 %copy-start.1 = (f32[16,128,128]{2,1,0:T(8,128)S(1)}, f32[16,128,128]{2,1,0:T(8,128)}, u32[]{:S(2)}) copy-start(f32[16,128,128]{2,1,0:T(8,128)} %fusion.1) | copy-start | bytes 3145732
where the time goes:
time: 119 us; the launch traced here: 117 us
  waiting for transfers between devices  38.3 us (32%)
  matrix products  34.9 us (29%)
  starting transfers between devices  21.5 us (18%)
  local copies, waits for them, and re-layouts  14.4 us (12%)
  other arithmetic  7.51 us (6%)
    ppermute x8, waiting for transfers between devices, partner(): lax.ppermute(x, axis, [(i, i ^ 1 << bit) for i in range(lax.axis_size(axi...  32.7 us
    dot_general x9, matrix products, near_term(): jnp.einsum('pq,bqc->bpc', node_mats[column], picked, preferred_element_ty...  13.3 us
    gather x9, local copies, waits for them, and re-layouts, near_term(): picked = jnp.take(mixed_rows, slot_rows[:, column], axis=0)  12.3 us
    dot_general x9, matrix products, near_term(): jnp.dot(flat_rows, chan_mats[column], preferred_element_type=jnp.float32)  11.7 us
    ppermute x8, starting transfers between devices, partner(): lax.ppermute(x, axis, [(i, i ^ 1 << bit) for i in range(lax.axis_size(axi...  9.48 us
    ppermute x4, starting transfers between devices, from_behind(): lax.ppermute(value, axis, [(source, source + steps) for source in range(i...  6.34 us
    ppermute x1, starting transfers between devices, padded(): before = lax.ppermute(last, axis, up)  4.43 us
    dot_general x4, matrix products, pick_matrices(): jnp.einsum('bs,spq->bpq', onehot, matrices.astype(jnp.float32))  3.97 us
  transfers between devices with their start and end apart: 14, of which 8 were waited for; matrix products, arithmetic and copies ran while one was open for 24% of the time, Pallas kernels for 0%

commit v1 on v0

v1 whole, which is shorter than its diff:
```python
import functools

import jax
import jax.numpy as jnp
from jax import lax
from jax.experimental import pallas as pl
from jax.experimental.pallas import tpu as pltpu
from jax.sharding import PartitionSpec as P

C = 128
BS = 128
KN = 3
BLK = 16
HALO = 4
HALF = BLK // 2
QTR = BLK // 4
F32 = jnp.float32
BF16 = jnp.bfloat16
MESH = pl.DeviceIdType.MESH
FORWARD = 4


def dot(a, b):
    return jnp.dot(a, b, preferred_element_type=F32)


def gelu(x):
    inner = 0.7978845608028654 * (x + 0.044715 * (x * x * x))
    return 0.5 * x * (1.0 + jnp.tanh(inner))


def kernel(
    n_dom,
    n_sub,
    feat_h,
    nf_h,
    nm_h,
    nt_h,
    rm_h,
    rt_h,
    nk_h,
    ck_h,
    rw_h,
    iw_h,
    sk_h,
    out_h,
    v0,
    nk,
    ck,
    rw,
    iw,
    sk,
    nf,
    nm,
    nt,
    rm,
    rt,
    h0,
    r1,
    ps,
    pf,
    pr,
    v1w,
    zr,
    v2w,
    y0,
    y1,
    y2,
    u0,
    u1,
    ob,
    in_sem,
    out_sem,
    core_sem,
    fine_sem,
    part_sem,
    zs_sem,
    v1x_sem,
    v1c_sem,
    rim_sem,
    rimc_sem,
    v2z_sem,
    v2x_sem,
    v2c_sem,
    v2r_sem,
):
    dom = lax.axis_index("dom")
    sub = lax.axis_index("sub")
    n1 = n_dom // 4
    n2 = n_dom // 16
    g1 = dom // 4
    g2 = dom // 16
    r = dom % 4
    c = r % 2
    xb = r // 2
    zi = g1 % 4
    core_dom = dom + 1 - 2 * c
    x_dom = dom + 2 - 4 * xb
    q0 = c * HALF + xb * QTR
    qx = c * HALF + (1 - xb) * QTR
    start0 = (dom * n_sub + sub) * BLK
    start1 = (g1 * n_sub + sub) * BLK
    start2 = (g2 * n_sub + sub) * BLK
    me = dom * n_sub + sub
    prev_ok = me > 0
    next_ok = me < n_dom * n_sub - 1
    prev_dom = (me + n_dom * n_sub - 1) % (n_dom * n_sub) // n_sub
    prev_sub = (sub + n_sub - 1) % n_sub
    next_dom = (me + 1) % (n_dom * n_sub) // n_sub
    next_sub = (sub + 1) % n_sub
    prev1 = g1 > 0
    next1 = g1 < n1 - 1
    prev2 = g2 > 0
    next2 = g2 < n2 - 1
    is_c1 = c == 1
    is_c0 = c == 0

    def z_dom(k):
        return dom + ((zi + k) % 4 - zi) * 4

    loads = [
        pltpu.make_async_copy(feat_h, v0, in_sem.at[0]),
        pltpu.make_async_copy(rw_h, rw, in_sem.at[1]),
        pltpu.make_async_copy(rm_h, rm, in_sem.at[2]),
        pltpu.make_async_copy(rt_h, rt, in_sem.at[3]),
        pltpu.make_async_copy(ck_h, ck, in_sem.at[4]),
        pltpu.make_async_copy(sk_h, sk, in_sem.at[5]),
        pltpu.make_async_copy(nf_h, nf, in_sem.at[6]),
        pltpu.make_async_copy(nm_h, nm, in_sem.at[7]),
        pltpu.make_async_copy(nt_h, nt, in_sem.at[8]),
        pltpu.make_async_copy(nk_h, nk, in_sem.at[9]),
        pltpu.make_async_copy(iw_h, iw, in_sem.at[10]),
    ]
    for copy in loads:
        copy.start()

    barrier = pltpu.get_barrier_semaphore()

    def greet(d, s):
        pl.semaphore_signal(barrier, inc=1, device_id={"dom": d, "sub": s}, device_id_type=MESH)

    greet(core_dom, sub)
    greet(x_dom, sub)
    for k in range(1, 4):
        greet(z_dom(k), sub)
    both = [
        (prev_ok, prev_dom, prev_sub),
        (next_ok, next_dom, next_sub),
    ]
    if n1 > 4:
        both += [(prev1, dom - 4, sub), (next1, dom + 4, sub)]
    if n2 > 1:
        both += [(prev2, dom - 16, sub), (next2, dom + 16, sub)]
    for ok, d, s in both:
        @pl.when(ok)
        def _(d=d, s=s):
            greet(d, s)
    expected = 5
    for ok, _, _ in both:
        expected = expected + jnp.where(ok, 1, 0)
    pl.semaphore_wait(barrier, expected)

    def remote(src, dst, sems, i, d, s=None):
        return pltpu.make_async_remote_copy(
            src_ref=src,
            dst_ref=dst,
            send_sem=sems.at[0, i],
            recv_sem=sems.at[1, i],
            device_id={"dom": d, "sub": sub if s is None else s},
            device_id_type=MESH,
        )

    def own_slot(kids, b, ident):
        s = jnp.where(kids[1, b] == ident, 1, 0)
        s = jnp.where(kids[2, b] == ident, 2, s)
        return jnp.where(kids[3, b] == ident, 3, s)

    def fine_slot(d, b):
        return own_slot(rm, start1 + b, (d * n_sub + sub) * BLK + b)

    def mid_slot(k, b):
        return own_slot(rt, start2 + b, ((g2 * 4 + k) * n_sub + sub) * BLK + b)

    def local(near, own, pitch):
        lower = near - (own - pitch) - (BLK - HALO)
        upper = near - (own + pitch) + HALO + BLK
        mine = near - own + HALO
        window = jnp.where(near < own, lower, jnp.where(near >= own + BLK, upper, mine))
        return jnp.clip(window, 0, BLK + 2 * HALO - 1)

    loads[0].wait()
    core = remote(v0.at[pl.ds((1 - c) * HALF, HALF)], r1, core_sem, 0, core_dom)
    core.start()
    up = remote(v0.at[pl.ds(BLK - HALO, HALO)], h0.at[pl.ds(0, HALO)], fine_sem, 0, next_dom, next_sub)
    down = remote(v0.at[pl.ds(0, HALO)], h0.at[pl.ds(HALO, HALO)], fine_sem, 1, prev_dom, prev_sub)

    @pl.when(next_ok)
    def _():
        up.start()

    @pl.when(prev_ok)
    def _():
        down.start()

    for copy in loads[1:]:
        copy.wait()

    def maps(level, src, dst, first, at, count):
        wide = jnp.concatenate([ck[level, 0], ck[level, 1], ck[level, 2]], axis=1)
        rows = src[pl.ds(first, count)].reshape(count * BS, C)
        dst[pl.ds(at, count)] = dot(rows, wide).astype(BF16).reshape(count, BS, KN * C)

    def own_maps(i, _):
        rows = v0[pl.ds(i * 4, 4)].reshape(4 * BS, C)
        left = jnp.concatenate([ck[0, 0], ck[0, 1]], axis=1)
        right = jnp.concatenate([ck[0, 2], sk[...]], axis=1)
        y0[pl.ds(HALO + i * 4, 4), :, pl.ds(0, 2 * C)] = dot(rows, left).astype(BF16).reshape(4, BS, 2 * C)
        got = dot(rows, right)
        y0[pl.ds(HALO + i * 4, 4), :, pl.ds(2 * C, C)] = got[:, :C].astype(BF16).reshape(4, BS, C)
        u0[pl.ds(i * 4, 4)] = got[:, C:].reshape(4, BS, C)
        return 0

    lax.fori_loop(0, 4, own_maps, 0, unroll=True)

    core.wait_recv()

    def chip_sum(b):
        mats = jnp.concatenate([rw[0, fine_slot(dom, b)], rw[0, fine_slot(core_dom, b)]], axis=1)
        vals = jnp.concatenate([v0[b], r1[b - c * HALF]], axis=0)
        return dot(mats, vals)

    part = [remote(ps.at[i], pr.at[i], part_sem, i, x_dom) for i in range(QTR)]
    for i in range(QTR):
        ps[i] = chip_sum(qx + i).astype(BF16)
        part[i].start()
    for i in range(QTR):
        pf[i] = chip_sum(q0 + i)

    @pl.when(prev_ok)
    def _():
        down.wait_send()

    @pl.when(next_ok)
    def _():
        up.wait_send()

    @pl.when(prev_ok)
    def _():
        up.wait_recv()
        rows = h0[pl.ds(0, HALO)].reshape(HALO * BS, C)
        y0[pl.ds(0, HALO), :, pl.ds(C, C)] = dot(rows, ck[0, 1]).astype(BF16).reshape(HALO, BS, C)

    @pl.when(next_ok)
    def _():
        down.wait_recv()
        rows = h0[pl.ds(HALO, HALO)].reshape(HALO * BS, C)
        y0[pl.ds(HALO + BLK, HALO), :, pl.ds(2 * C, C)] = dot(rows, ck[0, 2]).astype(BF16).reshape(HALO, BS, C)

    def near_pair(level, y, near, first, own, pitch, i):
        mats = jnp.concatenate([nk[level, 0], nk[level, 1], nk[level, 2]], axis=1)
        sides = []
        for b in (2 * i, 2 * i + 1):
            picks = [
                y[local(near[k, first + b], own, pitch), :, pl.ds(k * C, C)] for k in range(KN)
            ]
            sides.append(jnp.concatenate(picks, axis=0))
        got = dot(mats, jnp.concatenate(sides, axis=1))
        return got[:, :C], got[:, C:]

    def near_fine(i, _):
        one, two = near_pair(0, y0, nf, 0, start0, BLK, i)
        u0[2 * i] += one
        u0[2 * i + 1] += two
        return 0

    lax.fori_loop(0, BLK // 2, near_fine, 0, unroll=True)

    zsend = [
        remote(v1w.at[HALO + q0 + (zi + k) % 4], zr.at[k - 1], zs_sem, k - 1, z_dom(k))
        for k in range(1, 4)
    ]
    for i in range(QTR):
        part[i].wait_recv()
        v1w[HALO + q0 + i] = (pf[i] + pr[i].astype(F32)).astype(BF16)
    for copy in (zsend[1], zsend[0], zsend[2]):
        copy.start()
    own_quarter = v1w.at[pl.ds(HALO + q0, QTR)]
    other_quarter = v1w.at[pl.ds(HALO + qx, QTR)]
    v1x = remote(own_quarter, own_quarter, v1x_sem, 0, x_dom)
    v1x.start()
    v1c = [
        remote(own_quarter, own_quarter, v1c_sem, 0, core_dom),
        remote(other_quarter, other_quarter, v1c_sem, 1, core_dom),
    ]
    v1c[0].start()

    b2 = q0 + zi
    mine = dot(rw[1, mid_slot(zi, b2)], v1w[HALO + b2])
    for copy in zsend:
        copy.wait_recv()
    mats = [rw[1, mid_slot((zi + 4 - k) % 4, b2)] for k in range(1, 4)]
    vals = [zr[k - 1] for k in range(1, 4)]
    mine = mine + dot(jnp.concatenate(mats, axis=1), jnp.concatenate(vals, axis=0))
    v2w[HALO + b2] = mine.astype(BF16)

    def block2(b):
        return v2w.at[HALO + b]

    v2z = [remote(block2(b2), block2(b2), v2z_sem, k - 1, z_dom(k)) for k in range(1, 4)]
    for copy in (v2z[1], v2z[0], v2z[2]):
        copy.start()
    hops = [(zi + 4 - k) % 4 for k in range(4)]
    v2x = [remote(block2(q0 + h), block2(q0 + h), v2x_sem, k, x_dom) for k, h in enumerate(hops)]
    v2c = [remote(block2(q0 + h), block2(q0 + h), v2c_sem, k, core_dom) for k, h in enumerate(hops)]
    v2c += [remote(block2(qx + h), block2(qx + h), v2c_sem, 4 + k, core_dom) for k, h in enumerate(hops)]
    v2x[0].start()
    v2c[0].start()

    v1x.wait_recv()
    v1c[1].start()
    low = v1w.at[pl.ds(0, HALO)]
    high = v1w.at[pl.ds(HALO + BLK, HALO)]
    rim_up = remote(v1w.at[pl.ds(BLK, HALO)], low, rim_sem, 0, jnp.minimum(dom + 4, n_dom - 1))
    rim_down = remote(v1w.at[pl.ds(HALO, HALO)], high, rim_sem, 1, jnp.maximum(dom - 4, 0))
    low_core = remote(low, low, rimc_sem, 0, core_dom)
    high_core = remote(high, high, rimc_sem, 1, core_dom)

    @pl.when(is_c1 & next1)
    def _():
        rim_up.start()

    @pl.when(is_c0 & prev1)
    def _():
        rim_down.start()

    v1c[0].wait_recv()
    v1c[1].wait_recv()

    def mid_maps(i, _):
        maps(1, v1w, y1, HALO + i * 4, HALO + i * 4, 4)
        return 0

    lax.fori_loop(0, 4, mid_maps, 0, unroll=True)

    for k in (1, 3, 2):
        v2z[k - 1].wait_recv()
        v2x[k].start()
        v2c[k].start()

    @pl.when(is_c1 & prev1)
    def _():
        rim_up.wait_recv()
        low_core.start()

    @pl.when(is_c0 & next1)
    def _():
        rim_down.wait_recv()
        high_core.start()

    @pl.when(is_c0 & prev1)
    def _():
        low_core.wait_recv()

    @pl.when(is_c1 & next1)
    def _():
        high_core.wait_recv()

    @pl.when(prev1)
    def _():
        rows = v1w[pl.ds(0, HALO)].reshape(HALO * BS, C)
        y1[pl.ds(0, HALO), :, pl.ds(C, C)] = dot(rows, ck[1, 1]).astype(BF16).reshape(HALO, BS, C)

    @pl.when(next1)
    def _():
        rows = v1w[pl.ds(HALO + BLK, HALO)].reshape(HALO * BS, C)
        y1[pl.ds(HALO + BLK, HALO), :, pl.ds(2 * C, C)] = dot(rows, ck[1, 2]).astype(BF16).reshape(HALO, BS, C)

    def near_mid(i, _):
        one, two = near_pair(1, y1, nm, start1, start1, n_sub * BLK, i)
        u1[2 * i] = one
        u1[2 * i + 1] = two
        return 0

    lax.fori_loop(0, BLK // 2 - FORWARD, near_mid, 0, unroll=True)
    for k in (0, 1, 3, 2):
        v2x[k].wait_recv()
        v2c[4 + k].start()
    lax.fori_loop(BLK // 2 - FORWARD, BLK // 2, near_mid, 0, unroll=True)

    maps(2, v2w, y2, HALO + c * HALF, HALO + c * HALF, HALF)
    for k in range(2 * QTR):
        v2c[k].wait_recv()
    maps(2, v2w, y2, HALO + (1 - c) * HALF, HALO + (1 - c) * HALF, HALF)
    if n2 > 1:
        low2 = v2w.at[pl.ds(0, HALO)]
        high2 = v2w.at[pl.ds(HALO + BLK, HALO)]
        up2 = remote(v2w.at[pl.ds(BLK, HALO)], low2, v2r_sem, 0, jnp.minimum(dom + 16, n_dom - 1))
        down2 = remote(v2w.at[pl.ds(HALO, HALO)], high2, v2r_sem, 1, jnp.maximum(dom - 16, 0))

        @pl.when(next2)
        def _():
            up2.start()

        @pl.when(prev2)
        def _():
            down2.start()

        @pl.when(prev2)
        def _():
            up2.wait_recv()
            maps(2, v2w, y2, 0, 0, HALO)

        @pl.when(next2)
        def _():
            down2.wait_recv()
            maps(2, v2w, y2, HALO + BLK, HALO + BLK, HALO)

        @pl.when(next2)
        def _():
            up2.wait_send()

        @pl.when(prev2)
        def _():
            down2.wait_send()

    def out_copy(i):
        return pltpu.make_async_copy(ob.at[pl.ds(2 * i, 2)], out_h.at[pl.ds(2 * i, 2)], out_sem.at[i])

    def finish(i, _):
        sides = near_pair(2, y2, nt, start2, start2, n_sub * BLK, i)
        for b, side in zip((2 * i, 2 * i + 1), sides):
            mid = u1[b] + dot(iw[1, mid_slot(zi, b)], side.astype(BF16))
            fine = u0[b] + dot(iw[0, fine_slot(dom, b)], mid.astype(BF16))
            ob[b] = gelu(fine).astype(BF16)
        out_copy(i).start()
        return 0

    lax.fori_loop(0, BLK // 2, finish, 0, unroll=True)

    core.wait_send()
    for copy in part + zsend + [v1x] + v1c + v2z + v2x + v2c:
        copy.wait_send()

    @pl.when(is_c1 & next1)
    def _():
        rim_up.wait_send()

    @pl.when(is_c0 & prev1)
    def _():
        rim_down.wait_send()

    @pl.when(is_c1 & prev1)
    def _():
        low_core.wait_send()

    @pl.when(is_c0 & next1)
    def _():
        high_core.wait_send()

    for i in range(BLK // 2):
        out_copy(i).wait()


def shards(n_dom, n_sub, feat, near_fine, near_mid, near_top, restrict_mid, restrict_top, *weights):
    lists = [x.T for x in (near_fine, near_mid, near_top, restrict_mid, restrict_top)]
    any_spec = pl.BlockSpec(memory_space=pl.ANY)
    wide = HALO + BLK + HALO
    dma = pltpu.SemaphoreType.DMA
    vmem = pltpu.VMEM
    smem = pltpu.SMEM
    blocks = lambda n, kind=BF16, width=C: vmem((n, BS, width), kind)
    scratch = [
        blocks(BLK),
        vmem((3, KN, BS, BS), BF16),
        vmem((3, KN, C, C), BF16),
        vmem((2, 4, BS, BS), BF16),
        vmem((2, 4, BS, BS), BF16),
        vmem((C, C), BF16),
        *(smem(x.shape, jnp.int32) for x in lists),
        blocks(2 * HALO),
        blocks(HALF),
        blocks(QTR),
        blocks(QTR, F32),
        blocks(QTR),
        blocks(wide),
        blocks(3),
        blocks(wide),
        blocks(wide, BF16, KN * C),
        blocks(wide, BF16, KN * C),
        blocks(wide, BF16, KN * C),
        blocks(BLK, F32),
        blocks(BLK, F32),
        blocks(BLK),
        dma((11,)),
        dma((BLK // 2,)),
        dma((2, 1)),
        dma((2, 2)),
        dma((2, 4)),
        dma((2, 3)),
        dma((2, 1)),
        dma((2, 2)),
        dma((2, 2)),
        dma((2, 2)),
        dma((2, 3)),
        dma((2, 4)),
        dma((2, 8)),
        dma((2, 2)),
    ]
    out = pl.pallas_call(
        functools.partial(kernel, n_dom, n_sub),
        out_shape=jax.ShapeDtypeStruct((BLK, BS, C), BF16),
        in_specs=[pl.BlockSpec(memory_space=pltpu.HBM)] * 11,
        out_specs=any_spec,
        scratch_shapes=scratch,
        compiler_params=pltpu.CompilerParams(
            collective_id=0, has_side_effects=True, vmem_limit_bytes=62 * 2**20
        ),
    )(feat.reshape(BLK, BS, C), *lists, *weights)
    return out.reshape(BLK * BS, C)


def solution(mesh):
    rows = P(("dom", "sub"), None)
    in_specs = (rows, rows) + (P(),) * 9
    inner = functools.partial(shards, mesh.shape["dom"], mesh.shape["sub"])
    return jax.shard_map(inner, mesh=mesh, in_specs=in_specs, out_specs=rows, check_vma=False)
```

time: 119 us -> 33.8 us (0.28); the launches traced: 117 us -> 33.5 us
  waiting for transfers between devices: 38.3 us -> 0 us
  matrix products: 34.9 us -> 0 us
  Pallas kernels: 0 us -> 31.6 us
  starting transfers between devices: 21.5 us -> 0 us
  local copies, waits for them, and re-layouts: 14.4 us -> 1.87 us
  other arithmetic: 7.51 us -> 0 us
    ppermute x14 -> x0, waiting for transfers between devices: 38.3 us -> none  [the longest x8 32.7 us: partner(): lax.ppermute(x, axis, [(i, i ^ 1 << bit) for i in range(lax.axis_size(axi...]
    dot_general x26 -> x0, matrix products: 34.9 us -> none  [the longest x9 13.3 us: near_term(): jnp.einsum('pq,bqc->bpc', node_mats[column], picked, preferred_element_ty...]
    pallas_call x0 -> x1, Pallas kernels: none -> 31.6 us  [shards(): pl.pallas_call(functools.partial(kernel, n_dom, n_sub), out_shape=jax.Sha...]
    ppermute x14 -> x0, starting transfers between devices: 21.5 us -> none  [the longest x8 9.48 us: partner(): lax.ppermute(x, axis, [(i, i ^ 1 << bit) for i in range(lax.axis_size(axi...]
    gather x9 -> x0, local copies, waits for them, and re-layouts: 12.3 us -> none  [near_term(): picked = jnp.take(mixed_rows, slot_rows[:, column], axis=0)]
    select_n x11 -> x0, other arithmetic: 3.27 us -> none  [the longest x2 1.72 us: shards(): outgoing = jnp.where(first_bit == 0, upper_half, lower_half)]
    add x4 -> x0, other arithmetic: 2.31 us -> none  [the longest x2 2.3 us: shards(): jnp.where(first_bit == 0, lower_half, upper_half)]
  transfers between devices with their start and end apart: 14 -> 0, of which waited for: 8 -> 0; matrix products, arithmetic and copies ran while one was open for 24% -> 0% of each run, Pallas kernels for 0% -> 0%
where the time goes in v1:
time: 33.8 us; the launch traced here: 33.5 us
  Pallas kernels  31.6 us (93%)
  local copies, waits for them, and re-layouts  1.87 us (6%)
    pallas_call x1, Pallas kernels, shards(): pl.pallas_call(functools.partial(kernel, n_dom, n_sub), out_shape=jax.Sha...  31.6 us
    unnamed x1, local copies, waits for them, and re-layouts  1.87 us

profile of v1, /device:TPU:0, one launch (start us, length us, event | category | flops | bytes accessed | tf_op | source)
XLA Modules:
  0.0 33.5 jit_solution(1405472824371534765)
XLA Ops:
  0.0 31.6 %shard_map.109 = bf16[16,128,128]{2,1,0:T(8,128)(2,1)} custom-call(bf16[16,128,128]{2,1,0:T(8,128)(2,1)} %bitcast.8, s32[3,16]{1,0:T(4,128)} %bitcast.9, s32[3,128]{1,0:T(4,128)} %bitcast.10, s32[3,32]{1,0:T(4,128)} %bitcast.11, s32[4,128]{1,0:T(4,128)} %bitcast.12, s32[4,32]{1,0:T(4,128)} %bitcast.13, bf16[3,3,128,128]{3,2,1,0:T(8,128)(2,1)} %nk_h.1, ...), custom_call_target="tpu_custom_call" | custom-call | tf_op jit(solution)/shard_map/pallas_call | solution.py:509
  31.6 1.9 %copy.13 = bf16[2048,128]{1,0:T(8,128)(2,1)} copy(bf16[2048,128]{1,0:T(8,128)(2,1)} %bitcast.7) | data formatting | bytes 1048576

commit v2 on v1

--- a/solution.py
+++ b/solution.py
@@ -17,7 +17,6 @@
 F32 = jnp.float32
 BF16 = jnp.bfloat16
 MESH = pl.DeviceIdType.MESH
-FORWARD = 4
 
 
 def dot(a, b):
@@ -194,14 +193,6 @@
     up = remote(v0.at[pl.ds(BLK - HALO, HALO)], h0.at[pl.ds(0, HALO)], fine_sem, 0, next_dom, next_sub)
     down = remote(v0.at[pl.ds(0, HALO)], h0.at[pl.ds(HALO, HALO)], fine_sem, 1, prev_dom, prev_sub)
 
-    @pl.when(next_ok)
-    def _():
-        up.start()
-
-    @pl.when(prev_ok)
-    def _():
-        down.start()
-
     for copy in loads[1:]:
         copy.wait()
 
@@ -236,44 +227,32 @@
     for i in range(QTR):
         pf[i] = chip_sum(q0 + i)
 
+    @pl.when(next_ok)
+    def _():
+        up.start()
+
     @pl.when(prev_ok)
     def _():
-        down.wait_send()
-
-    @pl.when(next_ok)
-    def _():
-        up.wait_send()
-
-    @pl.when(prev_ok)
-    def _():
-        up.wait_recv()
-        rows = h0[pl.ds(0, HALO)].reshape(HALO * BS, C)
-        y0[pl.ds(0, HALO), :, pl.ds(C, C)] = dot(rows, ck[0, 1]).astype(BF16).reshape(HALO, BS, C)
-
-    @pl.when(next_ok)
-    def _():
-        down.wait_recv()
-        rows = h0[pl.ds(HALO, HALO)].reshape(HALO * BS, C)
-        y0[pl.ds(HALO + BLK, HALO), :, pl.ds(2 * C, C)] = dot(rows, ck[0, 2]).astype(BF16).reshape(HALO, BS, C)
-
-    def near_pair(level, y, near, first, own, pitch, i):
-        mats = jnp.concatenate([nk[level, 0], nk[level, 1], nk[level, 2]], axis=1)
+        down.start()
+
+    def near_pair(level, y, near, first, own, pitch, i, cols):
+        mats = jnp.concatenate([nk[level, k] for k in cols], axis=1)
         sides = []
         for b in (2 * i, 2 * i + 1):
             picks = [
-                y[local(near[k, first + b], own, pitch), :, pl.ds(k * C, C)] for k in range(KN)
+                y[local(near[k, first + b], own, pitch), :, pl.ds(k * C, C)] for k in cols
             ]
             sides.append(jnp.concatenate(picks, axis=0))
         got = dot(mats, jnp.concatenate(sides, axis=1))
         return got[:, :C], got[:, C:]
 
-    def near_fine(i, _):
-        one, two = near_pair(0, y0, nf, 0, start0, BLK, i)
+    def near_fine(cols, i, _):
+        one, two = near_pair(0, y0, nf, 0, start0, BLK, i, cols)
         u0[2 * i] += one
         u0[2 * i + 1] += two
         return 0
 
-    lax.fori_loop(0, BLK // 2, near_fine, 0, unroll=True)
+    lax.fori_loop(0, BLK // 2, functools.partial(near_fine, (0,)), 0, unroll=True)
 
     zsend = [
         remote(v1w.at[HALO + q0 + (zi + k) % 4], zr.at[k - 1], zs_sem, k - 1, z_dom(k))
@@ -294,6 +273,28 @@
     ]
     v1c[0].start()
 
+    @pl.when(prev_ok)
+    def _():
+        down.wait_send()
+
+    @pl.when(next_ok)
+    def _():
+        up.wait_send()
+
+    @pl.when(prev_ok)
+    def _():
+        up.wait_recv()
+        rows = h0[pl.ds(0, HALO)].reshape(HALO * BS, C)
+        y0[pl.ds(0, HALO), :, pl.ds(C, C)] = dot(rows, ck[0, 1]).astype(BF16).reshape(HALO, BS, C)
+
+    @pl.when(next_ok)
+    def _():
+        down.wait_recv()
+        rows = h0[pl.ds(HALO, HALO)].reshape(HALO * BS, C)
+        y0[pl.ds(HALO + BLK, HALO), :, pl.ds(2 * C, C)] = dot(rows, ck[0, 2]).astype(BF16).reshape(HALO, BS, C)
+
+    lax.fori_loop(0, BLK // 2, functools.partial(near_fine, (1, 2)), 0, unroll=True)
+
     b2 = q0 + zi
     mine = dot(rw[1, mid_slot(zi, b2)], v1w[HALO + b2])
     for copy in zsend:
@@ -342,6 +343,12 @@
 
     lax.fori_loop(0, 4, mid_maps, 0, unroll=True)
 
+    def near_mid_own(i, _):
+        u1[2 * i], u1[2 * i + 1] = near_pair(1, y1, nm, start1, start1, n_sub * BLK, i, (0,))
+        return 0
+
+    lax.fori_loop(0, BLK // 2, near_mid_own, 0, unroll=True)
+
     for k in (1, 3, 2):
         v2z[k - 1].wait_recv()
         v2x[k].start()
@@ -357,35 +364,36 @@
         rim_down.wait_recv()
         high_core.start()
 
-    @pl.when(is_c0 & prev1)
-    def _():
-        low_core.wait_recv()
-
-    @pl.when(is_c1 & next1)
-    def _():
-        high_core.wait_recv()
+    def rim_maps(at, k):
+        rows = v1w[pl.ds(at, HALO)].reshape(HALO * BS, C)
+        y1[pl.ds(at, HALO), :, pl.ds(k * C, C)] = dot(rows, ck[1, k]).astype(BF16).reshape(HALO, BS, C)
 
     @pl.when(prev1)
     def _():
-        rows = v1w[pl.ds(0, HALO)].reshape(HALO * BS, C)
-        y1[pl.ds(0, HALO), :, pl.ds(C, C)] = dot(rows, ck[1, 1]).astype(BF16).reshape(HALO, BS, C)
+        @pl.when(is_c0)
+        def _():
+            low_core.wait_recv()
+
+        rim_maps(0, 1)
 
     @pl.when(next1)
     def _():
-        rows = v1w[pl.ds(HALO + BLK, HALO)].reshape(HALO * BS, C)
-        y1[pl.ds(HALO + BLK, HALO), :, pl.ds(2 * C, C)] = dot(rows, ck[1, 2]).astype(BF16).reshape(HALO, BS, C)
-
-    def near_mid(i, _):
-        one, two = near_pair(1, y1, nm, start1, start1, n_sub * BLK, i)
-        u1[2 * i] = one
-        u1[2 * i + 1] = two
+        @pl.when(is_c1)
+        def _():
+            high_core.wait_recv()
+
+        rim_maps(HALO + BLK, 2)
+
+    def near_mid_rims(i, _):
+        one, two = near_pair(1, y1, nm, start1, start1, n_sub * BLK, i, (1, 2))
+        u1[2 * i] += one
+        u1[2 * i + 1] += two
         return 0
 
-    lax.fori_loop(0, BLK // 2 - FORWARD, near_mid, 0, unroll=True)
     for k in (0, 1, 3, 2):
         v2x[k].wait_recv()
         v2c[4 + k].start()
-    lax.fori_loop(BLK // 2 - FORWARD, BLK // 2, near_mid, 0, unroll=True)
+    lax.fori_loop(0, BLK // 2, near_mid_rims, 0, unroll=True)
 
     maps(2, v2w, y2, HALO + c * HALF, HALO + c * HALF, HALF)
     for k in range(2 * QTR):
@@ -424,18 +432,22 @@
             down2.wait_send()
 
     def out_copy(i):
-        return pltpu.make_async_copy(ob.at[pl.ds(2 * i, 2)], out_h.at[pl.ds(2 * i, 2)], out_sem.at[i])
+        return pltpu.make_async_copy(ob.at[pl.ds(4 * i, 4)], out_h.at[pl.ds(4 * i, 4)], out_sem.at[i])
 
     def finish(i, _):
-        sides = near_pair(2, y2, nt, start2, start2, n_sub * BLK, i)
-        for b, side in zip((2 * i, 2 * i + 1), sides):
-            mid = u1[b] + dot(iw[1, mid_slot(zi, b)], side.astype(BF16))
-            fine = u0[b] + dot(iw[0, fine_slot(dom, b)], mid.astype(BF16))
+        pairs = (2 * i, 2 * i + 1)
+        blks = [4 * i + n for n in range(4)]
+        sides = sum((near_pair(2, y2, nt, start2, start2, n_sub * BLK, j, (0, 1, 2)) for j in pairs), ())
+        sides = [side.astype(BF16) for side in sides]
+        mids = [u1[b] + dot(iw[1, mid_slot(zi, b)], side) for b, side in zip(blks, sides)]
+        mids = [mid.astype(BF16) for mid in mids]
+        fines = [u0[b] + dot(iw[0, fine_slot(dom, b)], mid) for b, mid in zip(blks, mids)]
+        for b, fine in zip(blks, fines):
             ob[b] = gelu(fine).astype(BF16)
         out_copy(i).start()
         return 0
 
-    lax.fori_loop(0, BLK // 2, finish, 0, unroll=True)
+    lax.fori_loop(0, BLK // 4, finish, 0, unroll=True)
 
     core.wait_send()
     for copy in part + zsend + [v1x] + v1c + v2z + v2x + v2c:
@@ -457,7 +469,7 @@
     def _():
         high_core.wait_send()
 
-    for i in range(BLK // 2):
+    for i in range(BLK // 4):
         out_copy(i).wait()
 
 
@@ -492,7 +504,7 @@
         blocks(BLK, F32),
         blocks(BLK),
         dma((11,)),
-        dma((BLK // 2,)),
+        dma((BLK // 4,)),
         dma((2, 1)),
         dma((2, 2)),
         dma((2, 4)),

time: 33.8 us -> 32.2 us (0.953)
  Pallas kernels: 31.6 us -> 30 us
    pallas_call x1, Pallas kernels: 31.6 us -> 30 us  [shards(): pl.pallas_call(functools.partial(kernel, n_dom, n_sub), out_shape=jax.Sha...]
where the time goes in v2:
time: 32.2 us; the launch traced here: 31.9 us
  Pallas kernels  30 us (93%)
  local copies, waits for them, and re-layouts  1.87 us (6%)
    pallas_call x1, Pallas kernels, shards(): pl.pallas_call(functools.partial(kernel, n_dom, n_sub), out_shape=jax.Sha...  30 us
    unnamed x1, local copies, waits for them, and re-layouts  1.87 us

profile of v2, /device:TPU:0, one launch (start us, length us, event | category | flops | bytes accessed | tf_op | source)
XLA Modules:
  0.0 31.9 jit_solution(12801174254699645752)
XLA Ops:
  0.0 30.0 %shard_map.109 = bf16[16,128,128]{2,1,0:T(8,128)(2,1)} custom-call(bf16[16,128,128]{2,1,0:T(8,128)(2,1)} %bitcast.8, s32[3,16]{1,0:T(4,128)} %bitcast.9, s32[3,128]{1,0:T(4,128)} %bitcast.10, s32[3,32]{1,0:T(4,128)} %bitcast.11, s32[4,128]{1,0:T(4,128)} %bitcast.12, s32[4,32]{1,0:T(4,128)} %bitcast.13, bf16[3,3,128,128]{3,2,1,0:T(8,128)(2,1)} %nk_h.1, ...), custom_call_target="tpu_custom_call" | custom-call | tf_op jit(solution)/shard_map/pallas_call | solution.py:521
  30.0 1.9 %copy.13 = bf16[2048,128]{1,0:T(8,128)(2,1)} copy(bf16[2048,128]{1,0:T(8,128)(2,1)} %bitcast.7) | data formatting | bytes 1048576

commit v3 on v2

--- a/solution.py
+++ b/solution.py
@@ -42,7 +42,7 @@
     rw_h,
     iw_h,
     sk_h,
-    out_h,
+    out,
     v0,
     nk,
     ck,
@@ -67,9 +67,7 @@
     y2,
     u0,
     u1,
-    ob,
     in_sem,
-    out_sem,
     core_sem,
     fine_sem,
     part_sem,
@@ -188,8 +186,14 @@
         return jnp.clip(window, 0, BLK + 2 * HALO - 1)
 
     loads[0].wait()
-    core = remote(v0.at[pl.ds((1 - c) * HALF, HALF)], r1, core_sem, 0, core_dom)
-    core.start()
+    core = []
+    for i, at in enumerate(((1 - xb) * QTR, xb * QTR)):
+        core.append(
+            remote(
+                v0.at[pl.ds((1 - c) * HALF + at, QTR)], r1.at[pl.ds(at, QTR)], core_sem, i, core_dom
+            )
+        )
+        core[i].start()
     up = remote(v0.at[pl.ds(BLK - HALO, HALO)], h0.at[pl.ds(0, HALO)], fine_sem, 0, next_dom, next_sub)
     down = remote(v0.at[pl.ds(0, HALO)], h0.at[pl.ds(HALO, HALO)], fine_sem, 1, prev_dom, prev_sub)
 
@@ -213,27 +217,22 @@
 
     lax.fori_loop(0, 4, own_maps, 0, unroll=True)
 
-    core.wait_recv()
+    core[0].wait_recv()
 
     def chip_sum(b):
         mats = jnp.concatenate([rw[0, fine_slot(dom, b)], rw[0, fine_slot(core_dom, b)]], axis=1)
         vals = jnp.concatenate([v0[b], r1[b - c * HALF]], axis=0)
         return dot(mats, vals)
 
-    part = [remote(ps.at[i], pr.at[i], part_sem, i, x_dom) for i in range(QTR)]
-    for i in range(QTR):
-        ps[i] = chip_sum(qx + i).astype(BF16)
-        part[i].start()
-    for i in range(QTR):
-        pf[i] = chip_sum(q0 + i)
-
-    @pl.when(next_ok)
-    def _():
-        up.start()
-
-    @pl.when(prev_ok)
-    def _():
-        down.start()
+    order = (2, 1, 3, 0)
+    turn = [(zi + k) % 4 for k in range(4)]
+    part = [remote(ps.at[k], pr.at[k], part_sem, k, x_dom) for k in range(QTR)]
+    for k in order:
+        ps[k] = chip_sum(qx + turn[k]).astype(BF16)
+        part[k].start()
+    core[1].wait_recv()
+    for k in order:
+        pf[k] = chip_sum(q0 + turn[k])
 
     def near_pair(level, y, near, first, own, pitch, i, cols):
         mats = jnp.concatenate([nk[level, k] for k in cols], axis=1)
@@ -255,14 +254,14 @@
     lax.fori_loop(0, BLK // 2, functools.partial(near_fine, (0,)), 0, unroll=True)
 
     zsend = [
-        remote(v1w.at[HALO + q0 + (zi + k) % 4], zr.at[k - 1], zs_sem, k - 1, z_dom(k))
+        remote(v1w.at[HALO + q0 + turn[k]], zr.at[k - 1], zs_sem, k - 1, z_dom(k))
         for k in range(1, 4)
     ]
-    for i in range(QTR):
-        part[i].wait_recv()
-        v1w[HALO + q0 + i] = (pf[i] + pr[i].astype(F32)).astype(BF16)
-    for copy in (zsend[1], zsend[0], zsend[2]):
-        copy.start()
+    for k in order:
+        part[k].wait_recv()
+        v1w[HALO + q0 + turn[k]] = (pf[k] + pr[k].astype(F32)).astype(BF16)
+        if k:
+            zsend[k - 1].start()
     own_quarter = v1w.at[pl.ds(HALO + q0, QTR)]
     other_quarter = v1w.at[pl.ds(HALO + qx, QTR)]
     v1x = remote(own_quarter, own_quarter, v1x_sem, 0, x_dom)
@@ -273,27 +272,13 @@
     ]
     v1c[0].start()
 
+    @pl.when(next_ok)
+    def _():
+        up.start()
+
     @pl.when(prev_ok)
     def _():
-        down.wait_send()
-
-    @pl.when(next_ok)
-    def _():
-        up.wait_send()
-
-    @pl.when(prev_ok)
-    def _():
-        up.wait_recv()
-        rows = h0[pl.ds(0, HALO)].reshape(HALO * BS, C)
-        y0[pl.ds(0, HALO), :, pl.ds(C, C)] = dot(rows, ck[0, 1]).astype(BF16).reshape(HALO, BS, C)
-
-    @pl.when(next_ok)
-    def _():
-        down.wait_recv()
-        rows = h0[pl.ds(HALO, HALO)].reshape(HALO * BS, C)
-        y0[pl.ds(HALO + BLK, HALO), :, pl.ds(2 * C, C)] = dot(rows, ck[0, 2]).astype(BF16).reshape(HALO, BS, C)
-
-    lax.fori_loop(0, BLK // 2, functools.partial(near_fine, (1, 2)), 0, unroll=True)
+        down.start()
 
     b2 = q0 + zi
     mine = dot(rw[1, mid_slot(zi, b2)], v1w[HALO + b2])
@@ -390,10 +375,31 @@
         u1[2 * i + 1] += two
         return 0
 
+    @pl.when(prev_ok)
+    def _():
+        down.wait_send()
+
+    @pl.when(next_ok)
+    def _():
+        up.wait_send()
+
+    @pl.when(prev_ok)
+    def _():
+        up.wait_recv()
+        rows = h0[pl.ds(0, HALO)].reshape(HALO * BS, C)
+        y0[pl.ds(0, HALO), :, pl.ds(C, C)] = dot(rows, ck[0, 1]).astype(BF16).reshape(HALO, BS, C)
+
+    @pl.when(next_ok)
+    def _():
+        down.wait_recv()
+        rows = h0[pl.ds(HALO, HALO)].reshape(HALO * BS, C)
+        y0[pl.ds(HALO + BLK, HALO), :, pl.ds(2 * C, C)] = dot(rows, ck[0, 2]).astype(BF16).reshape(HALO, BS, C)
+
     for k in (0, 1, 3, 2):
         v2x[k].wait_recv()
         v2c[4 + k].start()
     lax.fori_loop(0, BLK // 2, near_mid_rims, 0, unroll=True)
+    lax.fori_loop(0, BLK // 2, functools.partial(near_fine, (1, 2)), 0, unroll=True)
 
     maps(2, v2w, y2, HALO + c * HALF, HALO + c * HALF, HALF)
     for k in range(2 * QTR):
@@ -431,9 +437,6 @@
         def _():
             down2.wait_send()
 
-    def out_copy(i):
-        return pltpu.make_async_copy(ob.at[pl.ds(4 * i, 4)], out_h.at[pl.ds(4 * i, 4)], out_sem.at[i])
-
     def finish(i, _):
         pairs = (2 * i, 2 * i + 1)
         blks = [4 * i + n for n in range(4)]
@@ -443,14 +446,12 @@
         mids = [mid.astype(BF16) for mid in mids]
         fines = [u0[b] + dot(iw[0, fine_slot(dom, b)], mid) for b, mid in zip(blks, mids)]
         for b, fine in zip(blks, fines):
-            ob[b] = gelu(fine).astype(BF16)
-        out_copy(i).start()
+            out[b] = gelu(fine).astype(BF16)
         return 0
 
     lax.fori_loop(0, BLK // 4, finish, 0, unroll=True)
 
-    core.wait_send()
-    for copy in part + zsend + [v1x] + v1c + v2z + v2x + v2c:
+    for copy in core + part + zsend + [v1x] + v1c + v2z + v2x + v2c:
         copy.wait_send()
 
     @pl.when(is_c1 & next1)
@@ -468,14 +469,10 @@
     @pl.when(is_c0 & next1)
     def _():
         high_core.wait_send()
-
-    for i in range(BLK // 4):
-        out_copy(i).wait()
 
 
 def shards(n_dom, n_sub, feat, near_fine, near_mid, near_top, restrict_mid, restrict_top, *weights):
     lists = [x.T for x in (near_fine, near_mid, near_top, restrict_mid, restrict_top)]
-    any_spec = pl.BlockSpec(memory_space=pl.ANY)
     wide = HALO + BLK + HALO
     dma = pltpu.SemaphoreType.DMA
     vmem = pltpu.VMEM
@@ -502,10 +499,8 @@
         blocks(wide, BF16, KN * C),
         blocks(BLK, F32),
         blocks(BLK, F32),
-        blocks(BLK),
         dma((11,)),
-        dma((BLK // 4,)),
-        dma((2, 1)),
+        dma((2, 2)),
         dma((2, 2)),
         dma((2, 4)),
         dma((2, 3)),
@@ -520,9 +515,9 @@
     ]
     out = pl.pallas_call(
         functools.partial(kernel, n_dom, n_sub),
-        out_shape=jax.ShapeDtypeStruct((BLK, BS, C), BF16),
+        out_shape=pltpu.VMEM((BLK, BS, C), BF16),
         in_specs=[pl.BlockSpec(memory_space=pltpu.HBM)] * 11,
-        out_specs=any_spec,
+        out_specs=pl.BlockSpec(memory_space=pltpu.VMEM),
         scratch_shapes=scratch,
         compiler_params=pltpu.CompilerParams(
             collective_id=0, has_side_effects=True, vmem_limit_bytes=62 * 2**20

time: 32.2 us -> 28.2 us (0.88)
  Pallas kernels: 30 us -> 27.3 us
  local copies, waits for them, and re-layouts: 1.87 us -> 0.8 us
    pallas_call x1, Pallas kernels: 30 us -> 27.3 us  [shards(): pl.pallas_call(functools.partial(kernel, n_dom, n_sub), out_shape=pltpu.V...]
    unnamed x1, local copies, waits for them, and re-layouts: 1.87 us -> 0.8 us
where the time goes in v3:
time: 28.2 us; the launch traced here: 28.1 us
  Pallas kernels  27.3 us (97%)
  local copies, waits for them, and re-layouts  0.8 us (3%)
    pallas_call x1, Pallas kernels, shards(): pl.pallas_call(functools.partial(kernel, n_dom, n_sub), out_shape=pltpu.V...  27.3 us
    unnamed x1, local copies, waits for them, and re-layouts  0.8 us

profile of v3, /device:TPU:0, one launch (start us, length us, event | category | flops | bytes accessed | tf_op | source)
XLA Modules:
  0.0 28.1 jit_solution(17081404528945511615)
XLA Ops:
  0.0 27.3 %shard_map.109 = bf16[16,128,128]{2,1,0:T(8,128)(2,1)S(1)} custom-call(bf16[16,128,128]{2,1,0:T(8,128)(2,1)} %bitcast.8, s32[3,16]{1,0:T(4,128)} %bitcast.9, s32[3,128]{1,0:T(4,128)} %bitcast.10, s32[3,32]{1,0:T(4,128)} %bitcast.11, s32[4,128]{1,0:T(4,128)} %bitcast.12, s32[4,32]{1,0:T(4,128)} %bitcast.13, bf16[3,3,128,128]{3,2,1,0:T(8,128)(2,1)} %nk_h.1, ...), custom_call_target="tpu_custom_call" | custom-call | tf_op jit(solution)/shard_map/pallas_call | solution.py:516
  27.3 0.8 %copy.13 = bf16[2048,128]{1,0:T(8,128)(2,1)} copy(bf16[2048,128]{1,0:T(8,128)(2,1)S(1)} %bitcast.7) | data formatting | bytes 1048576
